TPU v7x, 128 devices: a whole 4x4x4 slice. The times are simulated.
128 devices in a mesh: section: 2 (over x_hi), row: 8 (over z, x_lo), col: 8 (over y, core).
Axes of the slice: x: 4 (x_hi: 2, x_lo: 2; x = x_hi * 2 + x_lo), y: 4, z: 4, core: 2. Of those that a mesh axis runs over, the one named last changes fastest.
Arguments:
- tokens: bfloat16 [2, 512, 12288], P('section', 'row', 'col'), may hold values from -6 to 6
- cotangent: bfloat16 [2, 512, 12288], P('section', 'row', 'col'), may hold values from -6 to 6
- w_in: bfloat16 [2, 12288, 24576], P('section', 'col', 'row'), may hold values from -0.0546875 to 0.0546875
- b_in: float32 [2, 24576], P('section', 'row'), may hold values from -3 to 3
- w_out: bfloat16 [2, 24576, 12288], P('section', 'row', 'col'), may hold values from -0.0390625 to 0.0390625
- b_out: float32 [2, 12288], P('section', 'col'), may hold values from -3 to 3
Outputs:
- handed_over: float32 [2, 512, 12288], P('section', 'row', 'col')
- leaving: bfloat16 [2, 512, 12288], P('section', 'row', 'col')
All inputs are finite; a program needn't handle non-finite values.
Results may differ from a plain program's by a relative error of at most 0.019.
Values may be sent and summed in bfloat16 or wider, within the bound.
A program may use at most 128 MiB of HBM per device.

v0:
```python
import math

import jax
import jax.numpy as jnp
from jax import lax
from jax.sharding import PartitionSpec as P

HB = 128


def swapped(value, axis, bit):
    mask = 2**bit
    pairs = [(source, source ^ mask) for source in range(lax.axis_size(axis))]
    return lax.ppermute(value, axis, pairs)


def hadamard_table(length):
    index = jnp.arange(length, dtype=jnp.int32)
    signs = jnp.ones((length, length), jnp.float32)
    level = 1
    while level < length:
        bit_set = index // level % 2
        signs = signs * (1.0 - 2.0 * (bit_set[:, None] * bit_set[None, :]).astype(jnp.float32))
        level = level * 2
    return signs / math.sqrt(length)


def rotate(field, rotation):
    blocks = field.reshape(field.shape[:-1] + (field.shape[-1] // HB, HB))
    turned = jnp.einsum("tbk,kj->tbj", blocks, rotation, precision=lax.Precision.HIGHEST)
    return turned.reshape(field.shape)


def gelu_parts(pre_act):
    factor = math.sqrt(2.0 / math.pi)
    tangent = jnp.tanh(factor * (pre_act + 0.044715 * pre_act * pre_act * pre_act))
    values = 0.5 * pre_act * (1.0 + tangent)
    slopes = 0.5 * (1.0 + tangent) + 0.5 * pre_act * (1.0 - tangent * tangent) * factor * (
        1.0 + 3.0 * 0.044715 * pre_act * pre_act
    )
    return (values, slopes)


def on_device(tokens, cotangent, w_in, b_in, w_out, b_out):
    section_id = lax.axis_index("section")
    tok_local = tokens[0]
    grad_local = cotangent[0]
    w_first = w_in[0]
    b_first = b_in[0]
    w_second = w_out[0]
    b_second = b_out[0]
    contract = (((1,), (1,)), ((), ()))
    tok_all = lax.all_gather(tok_local, "row", axis=0, tiled=True)
    picked = tok_all
    pre_act = (
        lax.psum_scatter(
            jnp.dot(picked, w_first, preferred_element_type=jnp.float32).astype(jnp.bfloat16),
            "col",
            scatter_dimension=0,
            tiled=True,
        ).astype(jnp.float32)
        + b_first
    )
    values, slopes = gelu_parts(pre_act)
    active_all = lax.all_gather(values.astype(jnp.bfloat16), "col", axis=0, tiled=True)
    picked = active_all
    output = (
        tok_local.astype(jnp.float32)
        + lax.psum_scatter(
            jnp.dot(picked, w_second, preferred_element_type=jnp.float32).astype(jnp.bfloat16),
            "row",
            scatter_dimension=0,
            tiled=True,
        ).astype(jnp.float32)
        + b_second
    )
    grad_all = lax.all_gather(grad_local, "row", axis=0, tiled=True)
    picked = grad_all
    back_sum = lax.psum_scatter(
        lax.dot_general(picked, w_second, contract, preferred_element_type=jnp.float32).astype(
            jnp.bfloat16
        ),
        "col",
        scatter_dimension=0,
        tiled=True,
    ).astype(jnp.float32)
    grad_hidden = lax.all_gather(
        (back_sum * slopes).astype(jnp.bfloat16), "col", axis=0, tiled=True
    )
    picked = grad_hidden
    grad_in = grad_local.astype(jnp.float32) + lax.psum_scatter(
        lax.dot_general(picked, w_first, contract, preferred_element_type=jnp.float32).astype(
            jnp.bfloat16
        ),
        "row",
        scatter_dimension=0,
        tiled=True,
    ).astype(jnp.float32)
    first_section = section_id == 0
    outgoing = jnp.where(first_section, output, grad_in)
    staying = jnp.where(first_section, grad_in, output)
    rotation = hadamard_table(HB)
    received = swapped(rotate(outgoing, rotation).astype(jnp.bfloat16), "section", 0)
    handed = rotate(received.astype(jnp.float32), rotation)
    return (handed[None], staying.astype(jnp.bfloat16)[None])


def solution(mesh):
    in_specs = (
        P("section", "row", "col"),
        P("section", "row", "col"),
        P("section", "col", "row"),
        P("section", "row"),
        P("section", "row", "col"),
        P("section", "col"),
    )
    out_specs = (P("section", "row", "col"), P("section", "row", "col"))
    return jax.shard_map(
        on_device, mesh=mesh, in_specs=in_specs, out_specs=out_specs, check_vma=False
    )
```

profile of v0, /device:TPU:0, one launch (start us, length us, event | category | flops | bytes accessed | tf_op | source)
XLA Modules:
  0.0 345.0 jit_solution(8982477197262215138)
XLA Ops:
  7.2 0.0 all-gather.11.cloned.1.call-start
  7.2 0.7 all-gather.11.cloned.1.call-update
  7.9 0.0 all-gather.13.cloned.1.call-start
  7.9 0.7 all-gather.13.cloned.1.call-update
  8.6 0.0 reduce-scatter.5.cloned.1.call-start
  8.7 47.2 %all-gather.11.cloned.1.call-done = bf16[1,512,1536]{2,1,0:T(8,128)(2,1)} async-done(((bf16[1,64,1536]{2,1,0:T(8,128)(2,1)}), bf16[1,512,1536]{2,1,0:T(8,128)(2,1)}) %all-gather.11.cloned.1.call-update) | async-done | bytes 1572880 | tf_op jit(solution)/shard_map/all_gather | solution.py:53
  55.8 9.3 %fusion.8 = bf16[512,3072]{1,0:T(8,128)(2,1)} fusion(bf16[1,1536,3072]{2,1,0:T(8,128)(2,1)} %param.8, bf16[1,512,1536]{2,1,0:T(8,128)(2,1)} %all-gather.11.cloned.1.call-done), kind=kOutput, calls=%fused_computation.8 | convolution fusion | flops 4833411072 | bytes 14155776 | tf_op jit(solution)/shard_map/dot_general | solution.py:57
  65.1 0.0 reduce-scatter.5.cloned.1.call-update
  65.1 0.0 reduce-scatter.9.cloned.1.call-start
  65.2 35.2 %all-gather.13.cloned.1.call-done = bf16[1,512,1536]{2,1,0:T(8,128)(2,1)} async-done(((bf16[1,64,1536]{2,1,0:T(8,128)(2,1)}), bf16[1,512,1536]{2,1,0:T(8,128)(2,1)}) %all-gather.13.cloned.1.call-update) | async-done | bytes 1572880 | tf_op jit(solution)/shard_map/all_gather | solution.py:77
  100.4 9.4 %fusion.11 = bf16[512,3072]{1,0:T(8,128)(2,1)} fusion(bf16[1,3072,1536]{2,1,0:T(8,128)(2,1)} %param.10, bf16[1,512,1536]{2,1,0:T(8,128)(2,1)} %all-gather.13.cloned.1.call-done), kind=kOutput, calls=%fused_computation.9 | convolution fusion | flops 4833411072 | bytes 14155776 | tf_op jit(solution)/shard_map/dot_general | solution.py:80
  109.8 0.0 copy-start.2
  109.8 0.0 reduce-scatter.9.cloned.1.call-update
  109.8 0.0 all-gather.9.cloned.1.call-start
  109.9 27.9 %reduce-scatter.5.cloned.1.call-done = bf16[64,3072]{1,0:T(8,128)(2,1)} async-done(((bf16[512,3072]{1,0:T(8,128)(2,1)}), bf16[64,3072]{1,0:T(8,128)(2,1)}) %reduce-scatter.5.cloned.1.call-update) | async-done | bytes 393232 | tf_op jit(solution)/shard_map/reduce_scatter | solution.py:56
  137.8 36.8 %reduce-scatter.9.cloned.1.call-done = bf16[64,3072]{1,0:T(8,128)(2,1)} async-done(((bf16[512,3072]{1,0:T(8,128)(2,1)}), bf16[64,3072]{1,0:T(8,128)(2,1)}) %reduce-scatter.9.cloned.1.call-update) | async-done | bytes 393232 | tf_op jit(solution)/shard_map/reduce_scatter | solution.py:79
  174.7 0.0 copy-done.2
  174.7 2.6 multiply_convert_fusion
  177.3 0.0 all-gather.9.cloned.1.call-update
  177.3 0.0 all-gather.7.cloned.1.call-start
  177.4 0.5 all-gather.7.cloned.1.call-update
  177.9 0.0 reduce-scatter.11.cloned.1.call-start
  177.9 26.1 %all-gather.9.cloned.1.call-done = bf16[512,3072]{1,0:T(8,128)(2,1)} async-done(((bf16[64,3072]{1,0:T(8,128)(2,1)}), bf16[512,3072]{1,0:T(8,128)(2,1)}) %all-gather.9.cloned.1.call-update) | async-done | bytes 3145744 | tf_op jit(solution)/shard_map/all_gather | solution.py:87
  204.0 10.3 %fusion.14 = bf16[512,1536]{1,0:T(8,128)(2,1)} fusion(bf16[512,3072]{1,0:T(8,128)(2,1)} %all-gather.9.cloned.1.call-done, bf16[1,1536,3072]{2,1,0:T(8,128)(2,1)} %param.8), kind=kOutput, calls=%fused_computation.10 | convolution fusion | flops 4832624640 | bytes 14155776 | tf_op jit(solution)/shard_map/dot_general | solution.py:92
  214.4 0.0 reduce-scatter.11.cloned.1.call-update
  214.4 0.0 copy-start.3
  214.4 0.0 copy-start
  214.4 0.0 copy-start.1
  214.4 0.0 reduce-scatter.7.cloned.1.call-start
  214.5 19.5 %all-gather.7.cloned.1.call-done = bf16[512,3072]{1,0:T(8,128)(2,1)} async-done(((bf16[64,3072]{1,0:T(8,128)(2,1)}), bf16[512,3072]{1,0:T(8,128)(2,1)}) %all-gather.7.cloned.1.call-update) | async-done | bytes 3145744 | tf_op jit(solution)/shard_map/all_gather | solution.py:65
  234.0 10.3 %fusion.17 = bf16[512,1536]{1,0:T(8,128)(2,1)} fusion(bf16[512,3072]{1,0:T(8,128)(2,1)} %all-gather.7.cloned.1.call-done, bf16[1,3072,1536]{2,1,0:T(8,128)(2,1)} %param.10), kind=kOutput, calls=%fused_computation.11 | convolution fusion | flops 4832624640 | bytes 14155776 | tf_op jit(solution)/shard_map/dot_general | solution.py:70
  244.2 0.0 reduce-scatter.7.cloned.1.call-update
  244.3 0.0 copy-done.3
  244.4 36.6 %reduce-scatter.11.cloned.1.call-done = bf16[64,1536]{1,0:T(8,128)(2,1)} async-done(((bf16[512,1536]{1,0:T(8,128)(2,1)}), bf16[64,1536]{1,0:T(8,128)(2,1)}) %reduce-scatter.11.cloned.1.call-update) | async-done | bytes 196624 | tf_op jit(solution)/shard_map/reduce_scatter | solution.py:91
  281.0 45.8 %reduce-scatter.7.cloned.1.call-done = bf16[64,1536]{1,0:T(8,128)(2,1)} async-done(((bf16[512,1536]{1,0:T(8,128)(2,1)}), bf16[64,1536]{1,0:T(8,128)(2,1)}) %reduce-scatter.7.cloned.1.call-update) | async-done | bytes 196624 | tf_op jit(solution)/shard_map/reduce_scatter | solution.py:69
  326.8 0.0 copy-done
  326.8 0.0 copy-done.1
  326.8 1.8 fusion.35
  328.6 0.6 fusion.22
  329.3 2.8 collective-permute-start
  332.1 4.4 %collective-permute-done = bf16[64,1536]{1,0:T(8,128)(2,1)S(1)} collective-permute-done((bf16[64,1536]{1,0:T(8,128)(2,1)S(1)}, bf16[64,1536]{1,0:T(8,128)(2,1)S(1)}, u32[]{:S(2)}, u32[]{:S(2)}) %collective-permute-start) | collective-permute-done | bytes 196640 | tf_op jit(solution)/shard_map/ppermute | solution.py:14
  336.6 0.5 fusion.36
  337.1 0.2 copy.12
  337.3 0.8 broadcast_in_dim_reshape.3
  (6 shorter events, 0.1 us)
Async XLA Ops:
  7.2 48.7 %all-gather.11.cloned.1.call-start = ((), (), s32[]{:S(2)}) async-start(), calls=%async_computation.10 | async-start | bytes 1769472 | tf_op jit(solution)/shard_map/all_gather | solution.py:53
  7.9 92.5 %all-gather.13.cloned.1.call-start = ((), (), s32[]{:S(2)}) async-start(), calls=%async_computation.11 | async-start | bytes 1769472 | tf_op jit(solution)/shard_map/all_gather | solution.py:77
  8.6 129.2 %reduce-scatter.5.cloned.1.call-start = ((), (), s32[]{:S(2)}) async-start(), calls=%async_computation.4 | async-start | bytes 3538944 | tf_op jit(solution)/shard_map/reduce_scatter | solution.py:56
  65.1 109.5 %reduce-scatter.9.cloned.1.call-start = ((), (), s32[]{:S(2)}) async-start(), calls=%async_computation.7 | async-start | bytes 3538944 | tf_op jit(solution)/shard_map/reduce_scatter | solution.py:79
  109.8 64.9 %copy-start.2 = (f32[1,3072]{1,0:T(1,128)S(1)}, f32[1,3072]{1,0:T(1,128)}, u32[]{:S(2)}) copy-start(f32[1,3072]{1,0:T(1,128)} %param.9) | copy-start | bytes 36868
  109.8 94.2 %all-gather.9.cloned.1.call-start = ((), (), s32[]{:S(2)}) async-start(), calls=%async_computation.8 | async-start | bytes 3538944 | tf_op jit(solution)/shard_map/all_gather | solution.py:87
  177.3 56.7 %all-gather.7.cloned.1.call-start = ((), (), s32[]{:S(2)}) async-start(), calls=%async_computation.5 | async-start | bytes 3538944 | tf_op jit(solution)/shard_map/all_gather | solution.py:65
  177.9 103.1 %reduce-scatter.11.cloned.1.call-start = ((), (), s32[]{:S(2)}) async-start(), calls=%async_computation.9 | async-start | bytes 1769472 | tf_op jit(solution)/shard_map/reduce_scatter | solution.py:91
  214.4 29.9 %copy-start.3 = (f32[1,1536]{1,0:T(1,128)S(1)}, f32[1,1536]{1,0:T(1,128)}, u32[]{:S(2)}) copy-start(f32[1,1536]{1,0:T(1,128)} %param.11) | copy-start | bytes 18436
  214.4 112.4 %copy-start = (bf16[1,64,1536]{2,1,0:T(8,128)(2,1)S(1)}, bf16[1,64,1536]{2,1,0:T(8,128)(2,1)}, u32[]{:S(2)}) copy-start(bf16[1,64,1536]{2,1,0:T(8,128)(2,1)} %param.6) | copy-start | bytes 589828
  214.4 112.4 %copy-start.1 = (bf16[1,64,1536]{2,1,0:T(8,128)(2,1)S(1)}, bf16[1,64,1536]{2,1,0:T(8,128)(2,1)}, u32[]{:S(2)}) copy-start(bf16[1,64,1536]{2,1,0:T(8,128)(2,1)} %param.7) | copy-start | bytes 589828
  214.4 112.4 %reduce-scatter.7.cloned.1.call-start = ((), (), s32[]{:S(2)}) async-start(), calls=%async_computation.6 | async-start | bytes 1769472 | tf_op jit(solution)/shard_map/reduce_scatter | solution.py:69
  329.3 7.3 %collective-permute-start = (bf16[64,1536]{1,0:T(8,128)(2,1)S(1)}, bf16[64,1536]{1,0:T(8,128)(2,1)S(1)}, u32[]{:S(2)}, u32[]{:S(2)}) collective-permute-start(bf16[64,1536]{1,0:T(8,128)(2,1)S(1)} %bitcast.59), channel_id=1, source_target_pairs={{0,64},{64,0},{1,65},{65,1},{2,66},{66,2},{3,67},{67,3},{4,68},{68... | collective-permute-start | bytes 589832 | tf_op jit(solution)/shard_map/ppermute | solution.py:14
Sparse Core Ops, SparseCore 0:
  9.6 46.1 all-gather.10
  57.5 42.8 all-gather.12
  102.8 34.9 reduce-scatter.4
  140.1 34.5 reduce-scatter.8
  177.4 26.5 all-gather.8
  206.2 27.7 all-gather.6
  236.4 44.5 reduce-scatter.10
  283.4 43.3 reduce-scatter.6
where the time goes:
time: 345 us
  waiting for transfers between devices  282 us (82%)
  matrix products  40.3 us (12%)
  between operations  14.2 us (4%)
  other arithmetic  4.49 us (1%)
    all_gather x1, waiting for transfers between devices, on_device(): tok_all = lax.all_gather(tok_local, 'row', axis=0, tiled=True)  47.2 us
    reduce_scatter x1, waiting for transfers between devices, on_device(): lax.psum_scatter(jnp.dot(picked, w_second, preferred_element_type=jnp.flo...  45.8 us
    reduce_scatter x1, waiting for transfers between devices, on_device(): lax.psum_scatter(lax.dot_general(picked, w_second, contract, preferred_el...  36.8 us
    reduce_scatter x1, waiting for transfers between devices, on_device(): lax.psum_scatter(lax.dot_general(picked, w_first, contract, preferred_ele...  36.6 us
    all_gather x1, waiting for transfers between devices, on_device(): grad_all = lax.all_gather(grad_local, 'row', axis=0, tiled=True)  35.2 us
    reduce_scatter x1, waiting for transfers between devices, on_device(): lax.psum_scatter(jnp.dot(picked, w_first, preferred_element_type=jnp.floa...  27.9 us
    all_gather x1, waiting for transfers between devices, on_device(): lax.all_gather((back_sum * slopes).astype(jnp.bfloat16), 'col', axis=0, t...  26.1 us
    all_gather x1, waiting for transfers between devices, on_device(): lax.all_gather(values.astype(jnp.bfloat16), 'col', axis=0, tiled=True)  19.5 us
  transfers between devices with their start and end apart: 9, of which 9 were waited for; matrix products, arithmetic and copies ran while one was open for 11% of the time, Pallas kernels for 0%

commit v1 on v0

v1 whole, which is shorter than its diff:
```python
import functools
import math

import jax
import jax.numpy as jnp
import numpy as np
from jax import lax
from jax.experimental import pallas as pl
from jax.experimental.pallas import tpu as pltpu
from jax.sharding import PartitionSpec as P

HB = 128
W = 1536
TN = 768
BF = jnp.bfloat16
F32 = jnp.float32


PAIRS = ((0, 32, 2, (1, 1)), (32, 32, 2, (2, 2)))
FORWARD, BACKWARD = 0, 1
GOES, STAYS = 0, 1
SEMAPHORES = 320

PHASES = (
    "ag1", "ag1b", "ag2a", "ag2b", "ag3", "ag4", "a1", "a2", "rs1", "rs2", "rs3", "yg1", "yg1b", "yg2", "yg3", "yg4",
    "b", "rr1", "rr2a", "rr2b", "rr3", "rr4", "fin",
)
ORDER = (
    0, 64, 96, 2, 32, 128, 66, 160, 8, 98, 192, 34, 130, 224, 256, 257, 72, 162, 194, 136, 40, 288, 104, 226, 289, 10,
    290, 259, 42, 258, 320, 168, 200, 291, 321, 74, 232, 138, 106, 322, 356, 296, 323, 297, 420, 357, 265, 359, 170,
    202, 234, 421, 264, 389, 267, 298, 266, 299, 388, 453, 485, 358, 329, 328, 330, 391, 452, 390, 484, 423, 422, 331,
    365, 364, 516, 397, 455, 487, 454, 396, 486, 428, 429, 548, 367, 366, 518, 398, 461, 612, 550, 460, 399, 492, 493,
    431, 430, 580, 524, 556, 557, 644, 588, 462, 494, 463, 495, 614, 582, 620, 589, 526, 652, 676, 590, 653, 621, 591,
    559, 558, 684, 622, 646, 623, 654, 685, 655, 708, 686, 678, 687, 716,
)


def hadamard_signs(length):
    index = np.arange(length)
    signs = np.ones((length, length), np.float32)
    level = 1
    while level < length:
        bit_set = index // level % 2
        signs = signs * (1.0 - 2.0 * (bit_set[:, None] * bit_set[None, :]))
        level = level * 2
    return signs


def gelu_parts(pre_act):
    factor = math.sqrt(2.0 / math.pi)
    tangent = jnp.tanh(factor * (pre_act + 0.044715 * pre_act * pre_act * pre_act))
    values = 0.5 * pre_act * (1.0 + tangent)
    slopes = 0.5 * (1.0 + tangent) + 0.5 * pre_act * (1.0 - tangent * tangent) * factor * (
        1.0 + 3.0 * 0.044715 * pre_act * pre_act
    )
    return (values, slopes)


def blocks_down(v):
    return jnp.concatenate([v[:, b * HB : (b + 1) * HB] for b in range(v.shape[1] // HB)], axis=0)


def blocks_back(v, rows):
    return jnp.concatenate([v[b * rows : (b + 1) * rows] for b in range(v.shape[0] // rows)], axis=1)


def turn(v, signs):
    return jnp.dot(v, signs, preferred_element_type=F32)


def pair_scratch(n):
    _, t, tiles, out_tiles = PAIRS[n]
    wide = W // tiles
    shapes = dict(
        x=pltpu.VMEM((2, 8 * t, W), BF),
        act=pltpu.VMEM((2, 2, tiles, 8 * t, wide), BF),
        slope=pltpu.VMEM((tiles, 2 * t, wide), F32),
        out=pltpu.VMEM((t, W), BF),
        inn=pltpu.VMEM((t, W), BF),
        ss=pltpu.VMEM((2, tiles, 8 * t, wide), BF),
        sr=pltpu.VMEM((2, tiles, 8 * t, wide), BF),
        c=pltpu.VMEM((2, tiles, 8 * t, wide), BF),
        ra=pltpu.VMEM((2, tiles, 2, t, wide), BF),
        rb=pltpu.VMEM((2, tiles, 2, 2 * t, wide), BF),
    )
    for slot, number in enumerate(out_tiles):
        wide = W // number
        shapes[f"p{slot}"] = pltpu.VMEM((number, 8 * t, wide), BF)
        shapes[f"rx{slot}"] = pltpu.VMEM((number, 2, t, wide), BF)
        shapes[f"rza{slot}"] = pltpu.VMEM((number, 2, t, wide), BF)
        shapes[f"rzb{slot}"] = pltpu.VMEM((number, 2, t, wide), BF)
        shapes[f"rh{slot}"] = pltpu.VMEM((number, t, wide), BF)
    return {f"{name}_{n}": shape for name, shape in shapes.items()}


def kernel(scratch_names, *refs):
    tok, cot, w1h, b_in, w2h, b_out, signs_ref, came, stayed = refs[:9]
    named = dict(zip(scratch_names, refs[9:], strict=True))
    w1, w2, w_sem, send, recv = (named[n] for n in ("w1", "w2", "w_sem", "send", "recv"))

    s, r, col = lax.axis_index("section"), lax.axis_index("row"), lax.axis_index("col")
    z, x, y, k = lax.div(r, 2), lax.rem(r, 2), lax.div(col, 2), lax.rem(col, 2)

    def row_id(dz, dx):
        return lax.rem(z + (dz + 4), 4) * 2 + (1 - x if dx else x)

    yp, ym, yo = lax.rem(y + 1, 4), lax.rem(y + 3, 4), lax.rem(y + 2, 4)
    to = {
        "z+": {"row": row_id(1, 0)},
        "z-": {"row": row_id(-1, 0)},
        "x": {"row": row_id(0, 1)},
        "y+": {"col": yp * 2 + k},
        "y-": {"col": ym * 2 + k},
        "k": {"col": y * 2 + 1 - k},
        "s": {"section": 1 - s},
    }

    indices, copies, pending = {}, {}, []

    def remote(name, src, dst, target):
        i = indices.setdefault(name, len(indices))
        assert i < SEMAPHORES
        return pltpu.make_async_remote_copy(
            src_ref=src,
            dst_ref=dst,
            send_sem=send.at[i],
            recv_sem=recv.at[i],
            device_id=to[target],
            device_id_type=pl.DeviceIdType.MESH,
        )

    def go(name, src, dst, target):
        copies[name] = remote(name, src, dst, target)
        copies[name].start()
        pending.append(copies[name])

    def got(*names):
        for name in names:
            if name in copies:
                copies.pop(name).wait_recv()

    loads = {}

    def load_weights(which, half):
        at = pl.multiple_of((k if half == 0 else 1 - k) * W, W)
        sem = w_sem.at[2 * (which - 1) + half]
        if which == 1:
            copy = pltpu.make_async_copy(w1h.at[0, :, pl.ds(at, W)], w1.at[half], sem)
        else:
            copy = pltpu.make_async_copy(w2h.at[0, pl.ds(at, W), :], w2.at[half], sem)
        copy.start()
        loads[which, half] = copy

    def need(which, half):
        copy = loads.pop((which, half), None)
        if copy is not None:
            copy.wait()

    def rows(index, size, part=None):
        start, count = (0, size) if part is None else part
        return pl.ds(pl.multiple_of(index * size + start, 16), count)

    def add_into(buf, first, others, count):
        @pl.loop(0, count // 16)
        def _(i):
            here = pl.ds(pl.multiple_of(first + i * 16, 16), 16)
            total = buf[here, :].astype(F32)
            for other, start in others:
                there = pl.ds(pl.multiple_of(start + i * 16, 16), 16)
                total = total + other[there, :].astype(F32)
            buf[here, :] = total.astype(BF)

    class Pair:
        def __init__(self, n):
            self.n = n
            self.first, self.t, self.tiles, self.out_tiles = PAIRS[n]
            self.wide = W // self.tiles
            for name in pair_scratch(n):
                setattr(self, name[: name.rindex("_")], named[name])

        def ways(self, odd):
            t = self.t
            if t >= 32:
                h = t // 2
                return (0, h), (h, t - h), (h, t - h), (0, h)
            return (None, (0, t), (0, t), None) if odd else ((0, t), None, None, (0, t))

    class Into:
        def __init__(self, pair, kind):
            self.q, self.kind = pair, kind
            self.forward = kind == FORWARD
            self.source = (tok if self.forward else cot).at[0]
            self.x = pair.x.at[kind]
            self.tag = f"i{pair.n}{kind}"
            self.up, self.up_rest, self.down, self.down_rest = pair.ways(not self.forward)

        def go(self, name, src, dst, target):
            go(self.tag + name, src, dst, target)

        def got(self, *names):
            got(*(self.tag + name for name in names))

        def part(self, p):
            return self.source.at[pl.ds(self.q.first + p[0], p[1])]

        def give(self, name, p, target):
            if p is not None:
                self.go(name, self.part(p), self.x.at[rows(row_id(0, 0), self.q.t, p)], target)

        def ag1(self, _):
            t = self.q.t
            self.give("x0", (0, t), "x")
            self.give("zpk", self.up, "z+")
            self.give("zmk", self.down, "z-")
            i = indices.setdefault(self.tag + "own", len(indices))
            self.own = pltpu.make_async_copy(
                self.part((0, t)), self.x.at[rows(row_id(0, 0), t)], send.at[i]
            )
            self.own.start()

        def ag1b(self, _):
            self.give("zpo", self.up_rest, "z+")
            self.give("zmo", self.down_rest, "z-")

        def pass_on(self, name, at, target):
            self.go(name, self.x.at[at], self.x.at[at], target)

        def ag2a(self, _):
            t = self.q.t
            if self.up is not None:
                self.got("zpk")
                self.pass_on("fp", rows(row_id(-1, 0), t, self.up), "z+")
            if self.down is not None:
                self.got("zmk")
                self.pass_on("fm", rows(row_id(1, 0), t, self.down), "z-")

        def ag2b(self, _):
            self.got("x0")
            peer = rows(row_id(0, 1), self.q.t)
            self.pass_on("zxp", peer, "z+")
            self.pass_on("zxm", peer, "z-")

        def ag3(self, _):
            self.got("fp", "fm")
            self.pass_on("x3", rows(row_id(2, 0), self.q.t), "x")

        def ag4(self, _):
            self.own.wait()
            self.got("zpo", "zmo", "zxp", "zxm", "x3")

        def into_hidden(self, half, tile, done):
            wide = self.q.wide
            for at in range(tile * wide, (tile + 1) * wide, TN):
                cols = pl.ds(at, TN)
                if self.forward:
                    value = jnp.dot(self.x[...], w1[half, :, cols], preferred_element_type=F32)
                else:
                    value = lax.dot_general(
                        self.x[...],
                        w2[half, cols, :],
                        (((1,), (1,)), ((), ())),
                        preferred_element_type=F32,
                    )
                done(pl.ds(at - tile * wide, TN), value)

        def a1(self, _):
            need(1 if self.forward else 2, 1)
            for tile in range(self.q.tiles):
                ss, sr = self.q.ss.at[self.kind, tile], self.q.sr.at[self.kind, tile]

                def done(cols, value):
                    ss[:, cols] = value.astype(BF)

                self.into_hidden(1, tile, done)
                self.go(f"ks{tile}", ss, sr, "k")

        def a2(self, _):
            need(1 if self.forward else 2, 0)
            t, size = self.q.t, 2 * self.q.t
            h0, h1 = (0, t), (t, t)
            for tile in range(self.q.tiles):
                c, sr = self.q.c.at[self.kind, tile], self.q.sr.at[self.kind, tile]
                ra = self.q.ra.at[self.kind, tile]
                self.got(f"ks{tile}")

                def done(cols, value):
                    c[:, cols] = (value + sr[:, cols].astype(F32)).astype(BF)

                self.into_hidden(0, tile, done)
                self.go(f"rap{tile}", c.at[rows(yo, size, h0)], ra.at[0], "y+")
                self.go(f"ram{tile}", c.at[rows(yo, size, h1)], ra.at[1], "y-")

        def rs1(self, tile):
            t, size = self.q.t, 2 * self.q.t
            c, rb = self.q.c.at[self.kind, tile], self.q.rb.at[self.kind, tile]
            self.go(f"rbpe{tile}", c.at[rows(yp, size, (t, t))], rb.at[0, pl.ds(t, t)], "y+")
            self.go(f"rbme{tile}", c.at[rows(ym, size, (0, t))], rb.at[1, pl.ds(0, t)], "y-")

        def rs2(self, tile):
            t, size = self.q.t, 2 * self.q.t
            c = self.q.c.at[self.kind, tile]
            ra, rb = self.q.ra.at[self.kind, tile], self.q.rb.at[self.kind, tile]
            self.got(f"rap{tile}")
            add_into(c, yp * size, [(ra.at[0], 0)], t)
            self.go(f"rbp{tile}", c.at[rows(yp, size, (0, t))], rb.at[0, pl.ds(0, t)], "y+")
            self.got(f"ram{tile}")
            add_into(c, ym * size + t, [(ra.at[1], 0)], t)
            self.go(f"rbm{tile}", c.at[rows(ym, size, (t, t))], rb.at[1, pl.ds(t, t)], "y-")

        def rs3(self, tile):
            size, wide = 2 * self.q.t, self.q.wide
            c, rb = self.q.c.at[self.kind, tile], self.q.rb.at[self.kind, tile]
            act, slope = self.q.act.at[self.kind, 0, tile], self.q.slope.at[tile]
            self.got(*(f"{name}{tile}" for name in ("rbpe", "rbme", "rbp", "rbm")))

            @pl.loop(0, size // 16)
            def _(i):
                here = pl.ds(pl.multiple_of(y * size + i * 16, 16), 16)
                piece = pl.ds(pl.multiple_of(i * 16, 16), 16)
                total = (
                    c[here, :].astype(F32) + rb[0, piece, :].astype(F32) + rb[1, piece, :].astype(F32)
                )
                if self.forward:
                    bias = b_in[:, pl.ds(pl.multiple_of(k * W + tile * wide, wide), wide)]
                    values, slopes = gelu_parts(total + bias)
                    slope[piece, :] = slopes
                else:
                    values = total * slope[piece, :]
                act[here, :] = values.astype(BF)

    class Out:
        def __init__(self, pair, slot):
            self.q, self.slot = pair, slot
            self.kind = s if slot == GOES else 1 - s
            self.act = pair.act.at[self.kind]
            self.number = pair.out_tiles[slot]
            self.wide = W // self.number
            self.p, self.rx, self.rza, self.rzb, self.rh = (
                getattr(pair, f"{name}{slot}") for name in ("p", "rx", "rza", "rzb", "rh")
            )
            self.tag = f"o{pair.n}{slot}"
            self.up, self.up_rest, self.down, self.down_rest = pair.ways(slot)

        def go(self, name, src, dst, target):
            go(self.tag + name, src, dst, target)

        def got(self, *names):
            got(*(self.tag + name for name in names))

        def yg1(self, tile):
            t, size = self.q.t, 2 * self.q.t
            h0, h1 = rows(y, size, (0, t)), rows(y, size, (t, t))
            self.pass_on(f"gp0{tile}", tile, h0, "y+")
            self.pass_on(f"gm1{tile}", tile, h1, "y-")

        def yg1b(self, tile):
            t, size = self.q.t, 2 * self.q.t
            h0, h1 = rows(y, size, (0, t)), rows(y, size, (t, t))
            self.pass_on(f"gp1{tile}", tile, h1, "y+")
            self.pass_on(f"gm0{tile}", tile, h0, "y-")
            self.across(f"k0{tile}", tile, rows(y, size))

        def pass_on(self, name, tile, at, target):
            mine = self.act.at[0, tile, at]
            self.go(name, mine, mine, target)

        def across(self, name, tile, at):
            self.go(name, self.act.at[0, tile, at], self.act.at[1, tile, at], "k")

        def yg2(self, tile):
            t, size = self.q.t, 2 * self.q.t
            self.got(f"gp0{tile}")
            self.pass_on(f"hp{tile}", tile, rows(ym, size, (0, t)), "y+")
            self.got(f"gm1{tile}")
            self.pass_on(f"hm{tile}", tile, rows(yp, size, (t, t)), "y-")

        def yg3(self, tile):
            size = 2 * self.q.t
            self.got(f"gp1{tile}")
            self.across(f"k1{tile}", tile, rows(ym, size))
            self.got(f"gm0{tile}")
            self.across(f"k2{tile}", tile, rows(yp, size))

        def yg4(self, tile):
            t, size = self.q.t, 2 * self.q.t
            self.got(f"hp{tile}")
            self.across(f"k3{tile}", tile, rows(yo, size, (0, t)))
            self.got(f"hm{tile}")
            self.across(f"k4{tile}", tile, rows(yo, size, (t, t)))

        def product(self, kind, half, at):
            cols, wide = pl.ds(at, TN), self.q.wide
            total = None
            for tile in range(self.q.tiles):
                hidden = pl.ds(tile * wide, wide)
                if kind == FORWARD:
                    value = jnp.dot(
                        self.act[half, tile], w2[half, hidden, cols], preferred_element_type=F32
                    )
                else:
                    value = lax.dot_general(
                        self.act[half, tile],
                        w1[half, cols, hidden],
                        (((1,), (1,)), ((), ())),
                        preferred_element_type=F32,
                    )
                total = value if total is None else total + value
            return total

        def b(self, _):
            for which in (1, 2):
                for half in (0, 1):
                    need(which, half)
            for tile in range(self.q.tiles):
                self.got(*(f"k{i}{tile}" for i in range(5)))
            for out in range(self.number):
                p = self.p.at[out]

                def tile_of(kind):
                    for at in range(out * self.wide, (out + 1) * self.wide, TN):
                        total = self.product(kind, 0, at) + self.product(kind, 1, at)
                        p[:, pl.ds(at - out * self.wide, TN)] = total.astype(BF)

                pl.when(self.kind == FORWARD)(functools.partial(tile_of, FORWARD))
                pl.when(self.kind == BACKWARD)(functools.partial(tile_of, BACKWARD))
                t = self.q.t
                self.go(f"x1{out}", p.at[rows(row_id(2, 1), t)], self.rx.at[out, 0], "x")
                self.go(f"zap{out}", p.at[rows(row_id(1, 1), t)], self.rza.at[out, 0], "z+")
                self.go(f"zam{out}", p.at[rows(row_id(-1, 1), t)], self.rza.at[out, 1], "z-")

        def rr1(self, out):
            self.give_sum(f"zbpe{out}", out, row_id(1, 0), self.up_rest, 0, "z+")
            self.give_sum(f"zbme{out}", out, row_id(-1, 0), self.down_rest, 1, "z-")

        def give_sum(self, name, out, row, part, side, target):
            if part is not None:
                self.go(
                    name,
                    self.p.at[out, rows(row, self.q.t, part)],
                    self.rzb.at[out, side, pl.ds(*part)],
                    target,
                )

        def rr2a(self, out):
            t, p, far = self.q.t, self.p.at[out], row_id(2, 0)
            self.got(f"x1{out}")
            add_into(p, far * t, [(self.rx.at[out, 0], 0)], t)
            for name, part, target in (("zhp", self.up, "z+"), ("zhm", self.down, "z-")):
                if part is not None:
                    self.go(f"{name}{out}", p.at[rows(far, t, part)], self.rh.at[out, pl.ds(*part)], target)

        def rr2b(self, out):
            t, p, peer = self.q.t, self.p.at[out], row_id(0, 1)
            self.got(f"zap{out}", f"zam{out}")
            add_into(p, peer * t, [(self.rza.at[out, 0], 0), (self.rza.at[out, 1], 0)], t)
            self.go(f"x2{out}", p.at[rows(peer, t)], self.rx.at[out, 1], "x")

        def rr3(self, out):
            t, p, rh = self.q.t, self.p.at[out], self.rh.at[out]
            if self.up is not None:
                self.got(f"zhp{out}")
                add_into(p, row_id(1, 0) * t + self.up[0], [(rh, self.up[0])], self.up[1])
                self.give_sum(f"zbp{out}", out, row_id(1, 0), self.up, 0, "z+")
            if self.down is not None:
                self.got(f"zhm{out}")
                add_into(p, row_id(-1, 0) * t + self.down[0], [(rh, self.down[0])], self.down[1])
                self.give_sum(f"zbm{out}", out, row_id(-1, 0), self.down, 1, "z-")

        def rr4(self, out):
            t, wide = self.q.t, self.wide
            self.got(*(f"{name}{out}" for name in ("zbpe", "zbme", "zbp", "zbm", "x2")))
            mine = rows(row_id(0, 0), t)
            cols = pl.ds(out * wide, wide)
            total = (
                self.p[out, mine, :].astype(F32)
                + self.rzb[out, 0].astype(F32)
                + self.rzb[out, 1].astype(F32)
                + self.rx[out, 1].astype(F32)
                + self.q.x[self.kind, mine, cols].astype(F32)
            )
            total = total + jnp.where(self.kind == FORWARD, b_out[:, cols], 0.0)
            if self.slot == STAYS:
                stayed[pl.ds(self.q.first, t), cols] = total.astype(BF)
                return
            stacked = blocks_down(total)
            high = stacked.astype(BF)
            rest = stacked - high.astype(F32)
            mid = rest.astype(BF)
            low = (rest - mid.astype(F32)).astype(BF)
            signs = signs_ref[...]
            turned = turn(high, signs) + (turn(mid, signs) + turn(low, signs))
            turned = turned * (1.0 / math.sqrt(HB))
            self.q.out[:, cols] = blocks_back(turned, t).astype(BF)
            self.go(f"sec{out}", self.q.out.at[:, cols], self.q.inn.at[:, cols], "s")

        def fin(self, _):
            self.got(*(f"sec{out}" for out in range(self.number)))
            came[pl.ds(self.q.first, self.q.t), :] = self.q.inn[...]

    for which, half in ((1, 1), (1, 0), (2, 1), (2, 0)):
        load_weights(which, half)

    barrier = pltpu.get_barrier_semaphore()
    for target in to.values():
        pl.semaphore_signal(barrier, inc=1, device_id=target, device_id_type=pl.DeviceIdType.MESH)
    pl.semaphore_wait(barrier, len(to))

    jobs = []
    for n in range(len(PAIRS)):
        pair = Pair(n)
        jobs.append((Into(pair, FORWARD), Into(pair, BACKWARD), Out(pair, GOES), Out(pair, STAYS)))
    for step in ORDER:
        phase, job = PHASES[step // 32], jobs[step // 8 % 4][step // 2 % 4]
        getattr(job, phase)(step % 2)
    for copy in pending:
        copy.wait_send()


def finish_kernel(came, stayed, signs, handed, leaving):
    turned = turn(blocks_down(came[...]), signs[...]) * (1.0 / math.sqrt(HB))
    handed[0] = blocks_back(turned, came.shape[0])
    leaving[0] = stayed[...]


def on_device(tokens, cotangent, w_in, b_in, w_out, b_out):
    scratch = dict(
        w1=pltpu.VMEM((2, W, W), BF),
        w2=pltpu.VMEM((2, W, W), BF),
        w_sem=pltpu.SemaphoreType.DMA((4,)),
        send=pltpu.SemaphoreType.DMA((SEMAPHORES,)),
        recv=pltpu.SemaphoreType.DMA((SEMAPHORES,)),
    )
    for n in range(len(PAIRS)):
        scratch.update(pair_scratch(n))
    signs = jnp.asarray(hadamard_signs(HB), BF)
    vmem, anywhere = pl.BlockSpec(memory_space=pltpu.VMEM), pl.BlockSpec(memory_space=pl.ANY)
    tile = jax.ShapeDtypeStruct(tokens.shape[1:], BF)
    came, stayed = pl.pallas_call(
        functools.partial(kernel, tuple(scratch)),
        out_shape=(tile, tile),
        in_specs=[anywhere, anywhere, anywhere, vmem, anywhere, vmem, vmem],
        out_specs=(vmem, vmem),
        scratch_shapes=list(scratch.values()),
        cost_estimate=pl.CostEstimate(flops=19_500_000_000, bytes_accessed=20_000_000, transcendentals=200_000),
        compiler_params=pltpu.CompilerParams(
            collective_id=0, has_side_effects=True, vmem_limit_bytes=56 << 20
        ),
        name="feed_forward",
    )(tokens, cotangent, w_in, b_in, w_out, b_out, signs)
    return pl.pallas_call(
        finish_kernel,
        out_shape=(
            jax.ShapeDtypeStruct(tokens.shape, F32),
            jax.ShapeDtypeStruct(tokens.shape, BF),
        ),
        in_specs=[vmem, vmem, vmem],
        out_specs=(vmem, vmem),
        name="hand_over",
    )(came, stayed, signs)


def solution(mesh):
    in_specs = (
        P("section", "row", "col"),
        P("section", "row", "col"),
        P("section", "col", "row"),
        P("section", "row"),
        P("section", "row", "col"),
        P("section", "col"),
    )
    out_specs = (P("section", "row", "col"), P("section", "row", "col"))
    return jax.shard_map(
        on_device, mesh=mesh, in_specs=in_specs, out_specs=out_specs, check_vma=False
    )
```

time: 345 us -> 107 us (0.31)
  waiting for transfers between devices: 282 us -> 0 us
  Pallas kernels: 0 us -> 106 us
  matrix products: 40.3 us -> 0 us
  between operations: 14.2 us -> 0.64 us
  other arithmetic: 4.49 us -> 0 us
    reduce_scatter x4 -> x0, waiting for transfers between devices: 147 us -> none  [the longest x1 45.8 us: on_device(): lax.psum_scatter(jnp.dot(picked, w_second, preferred_element_type=jnp.flo...]
    all_gather x4 -> x0, waiting for transfers between devices: 128 us -> none  [the longest x1 47.2 us: on_device(): tok_all = lax.all_gather(tok_local, 'row', axis=0, tiled=True)]
    pallas_call x0 -> x2, Pallas kernels: none -> 106 us  [the longest x1 105 us: on_device(): pl.pallas_call(functools.partial(kernel, tuple(scratch)), out_shape=(tile...]
    dot_general x6 -> x0, matrix products: 40.3 us -> none  [the longest x1 10.3 us: on_device(): lax.dot_general(picked, w_first, contract, preferred_element_type=jnp.flo...]
    ppermute x1 -> x0, waiting for transfers between devices: 4.45 us -> none  [swapped(): return lax.ppermute(value, axis, pairs)]
  transfers between devices with their start and end apart: 9 -> 0, of which waited for: 9 -> 0; matrix products, arithmetic and copies ran while one was open for 11% -> 0% of each run, Pallas kernels for 0% -> 0%
where the time goes in v1:
time: 107 us
  Pallas kernels  106 us (99%)
    pallas_call x1, Pallas kernels, on_device(): pl.pallas_call(functools.partial(kernel, tuple(scratch)), out_shape=(tile...  105 us

profile of v1, /device:TPU:0, one launch (start us, length us, event | category | flops | bytes accessed | tf_op | source)
XLA Modules:
  0.0 107.1 jit_solution(6191775630582960849)
XLA Ops:
  0.6 104.5 %feed_forward.1 = (bf16[64,1536]{1,0:T(8,128)(2,1)}, bf16[64,1536]{1,0:T(8,128)(2,1)}) custom-call(bf16[1,64,1536]{2,1,0:T(8,128)(2,1)} %refs_0_.1, bf16[1,64,1536]{2,1,0:T(8,128)(2,1)} %refs_1_.1, bf16[1,1536,3072]{2,1,0:T(8,128)(2,1)} %refs_2_.1, f32[1,3072]{1,0:T(1,128)} %refs_3_.1, bf16[1,3072,1536]{2,1,0:T(8,128)(2,1)} %refs_4_.1, f32[1,1536]{1,0:T(1,128)} %refs_5_.1, ...), custom_call_target="tpu_custom_call" | custom-call | flops 19499999232 | bytes 20000000 | tf_op jit(solution)/shard_map/feed_forward/pallas_call | solution.py:538
  105.2 2.0 %hand_over.1 = (f32[1,64,1536]{2,1,0:T(8,128)}, bf16[1,64,1536]{2,1,0:T(8,128)(2,1)}) custom-call(bf16[64,1536]{1,0:T(8,128)(2,1)} %get-tuple-element.4.came, bf16[64,1536]{1,0:T(8,128)(2,1)} %get-tuple-element.5.stayed, bf16[128,128]{1,0:T(8,128)(2,1)} %constant.2.clone.refs_6_.signs), custom_call_target="tpu_custom_call" | custom-call | tf_op jit(solution)/shard_map/hand_over/pallas_call | solution.py:550

commit v2 on v1

--- a/solution.py
+++ b/solution.py
@@ -16,7 +16,7 @@
 F32 = jnp.float32
 
 
-PAIRS = ((0, 32, 2, (1, 1)), (32, 32, 2, (2, 2)))
+PAIRS = ((0, 32, 2, (1, 1), True, (False, False)), (32, 32, 1, (2, 2), False, (True, True)))
 FORWARD, BACKWARD = 0, 1
 GOES, STAYS = 0, 1
 SEMAPHORES = 320
@@ -26,12 +26,12 @@
     "b", "rr1", "rr2a", "rr2b", "rr3", "rr4", "fin",
 )
 ORDER = (
-    0, 64, 96, 2, 32, 128, 66, 160, 8, 98, 192, 34, 130, 224, 256, 257, 72, 162, 194, 136, 40, 288, 104, 226, 289, 10,
-    290, 259, 42, 258, 320, 168, 200, 291, 321, 74, 232, 138, 106, 322, 356, 296, 323, 297, 420, 357, 265, 359, 170,
-    202, 234, 421, 264, 389, 267, 298, 266, 299, 388, 453, 485, 358, 329, 328, 330, 391, 452, 390, 484, 423, 422, 331,
-    365, 364, 516, 397, 455, 487, 454, 396, 486, 428, 429, 548, 367, 366, 518, 398, 461, 612, 550, 460, 399, 492, 493,
-    431, 430, 580, 524, 556, 557, 644, 588, 462, 494, 463, 495, 614, 582, 620, 589, 526, 652, 676, 590, 653, 621, 591,
-    559, 558, 684, 622, 646, 623, 654, 685, 655, 708, 686, 678, 687, 716,
+    0, 64, 32, 2, 128, 66, 96, 34, 98, 130, 10, 160, 193, 192, 225, 224, 162, 195, 256, 8, 257, 74, 42, 227, 259, 106,
+    288, 194, 289, 138, 72, 291, 226, 258, 321, 40, 323, 357, 359, 104, 320, 136, 170, 391, 389, 202, 290, 421, 234,
+    266, 168, 200, 322, 356, 453, 485, 358, 232, 420, 388, 264, 296, 298, 452, 423, 484, 390, 455, 422, 516, 328, 330,
+    364, 396, 487, 454, 486, 580, 612, 548, 428, 366, 518, 460, 492, 398, 644, 550, 524, 430, 582, 556, 525, 557, 462,
+    614, 676, 494, 620, 646, 588, 652, 526, 621, 589, 527, 653, 708, 558, 622, 590, 678, 684, 685, 591, 623, 559, 654,
+    686, 716, 655, 687,
 )
 
 
@@ -69,7 +69,7 @@
 
 
 def pair_scratch(n):
-    _, t, tiles, out_tiles = PAIRS[n]
+    _, t, tiles, out_tiles, _, _ = PAIRS[n]
     wide = W // tiles
     shapes = dict(
         x=pltpu.VMEM((2, 8 * t, W), BF),
@@ -101,18 +101,24 @@
     s, r, col = lax.axis_index("section"), lax.axis_index("row"), lax.axis_index("col")
     z, x, y, k = lax.div(r, 2), lax.rem(r, 2), lax.div(col, 2), lax.rem(col, 2)
 
+    row_ids = {}
+    for dz in (0, 1, -1, 2):
+        for dx in (0, 1):
+            row_ids[dz, dx] = lax.rem(z + (dz + 4), 4) * 2 + (1 - x if dx else x)
+
     def row_id(dz, dx):
-        return lax.rem(z + (dz + 4), 4) * 2 + (1 - x if dx else x)
+        return row_ids[dz, dx]
 
     yp, ym, yo = lax.rem(y + 1, 4), lax.rem(y + 3, 4), lax.rem(y + 2, 4)
     to = {
-        "z+": {"row": row_id(1, 0)},
-        "z-": {"row": row_id(-1, 0)},
-        "x": {"row": row_id(0, 1)},
-        "y+": {"col": yp * 2 + k},
-        "y-": {"col": ym * 2 + k},
-        "k": {"col": y * 2 + 1 - k},
-        "s": {"section": 1 - s},
+        "z+": (s, row_id(1, 0), col),
+        "z-": (s, row_id(-1, 0), col),
+        "z2": (s, row_id(2, 0), col),
+        "x": (s, row_id(0, 1), col),
+        "y+": (s, r, yp * 2 + k),
+        "y-": (s, r, ym * 2 + k),
+        "k": (s, r, y * 2 + 1 - k),
+        "s": (1 - s, r, col),
     }
 
     indices, copies, pending = {}, {}, []
@@ -139,6 +145,12 @@
             if name in copies:
                 copies.pop(name).wait_recv()
 
+    def settle(keep):
+        sent = pending[: max(0, len(pending) - keep)]
+        del pending[: len(sent)]
+        for copy in sent:
+            copy.wait_send()
+
     loads = {}
 
     def load_weights(which, half):
@@ -173,13 +185,15 @@
     class Pair:
         def __init__(self, n):
             self.n = n
-            self.first, self.t, self.tiles, self.out_tiles = PAIRS[n]
+            self.first, self.t, self.tiles, self.out_tiles, self.straight, self.out_straight = PAIRS[n]
             self.wide = W // self.tiles
             for name in pair_scratch(n):
                 setattr(self, name[: name.rindex("_")], named[name])
 
-        def ways(self, odd):
+        def ways(self, odd, straight):
             t = self.t
+            if straight:
+                return None, (0, t), None, (0, t)
             if t >= 32:
                 h = t // 2
                 return (0, h), (h, t - h), (h, t - h), (0, h)
@@ -192,7 +206,7 @@
             self.source = (tok if self.forward else cot).at[0]
             self.x = pair.x.at[kind]
             self.tag = f"i{pair.n}{kind}"
-            self.up, self.up_rest, self.down, self.down_rest = pair.ways(not self.forward)
+            self.up, self.up_rest, self.down, self.down_rest = pair.ways(not self.forward, pair.straight)
 
         def go(self, name, src, dst, target):
             go(self.tag + name, src, dst, target)
@@ -210,6 +224,8 @@
         def ag1(self, _):
             t = self.q.t
             self.give("x0", (0, t), "x")
+            if self.q.straight:
+                self.give("z2", (0, t), "z2")
             self.give("zpk", self.up, "z+")
             self.give("zmk", self.down, "z-")
             i = indices.setdefault(self.tag + "own", len(indices))
@@ -241,7 +257,7 @@
             self.pass_on("zxm", peer, "z-")
 
         def ag3(self, _):
-            self.got("fp", "fm")
+            self.got("fp", "fm", "z2")
             self.pass_on("x3", rows(row_id(2, 0), self.q.t), "x")
 
         def ag4(self, _):
@@ -263,32 +279,28 @@
                     )
                 done(pl.ds(at - tile * wide, TN), value)
 
-        def a1(self, _):
+        def a1(self, tile):
             need(1 if self.forward else 2, 1)
-            for tile in range(self.q.tiles):
-                ss, sr = self.q.ss.at[self.kind, tile], self.q.sr.at[self.kind, tile]
-
-                def done(cols, value):
-                    ss[:, cols] = value.astype(BF)
-
-                self.into_hidden(1, tile, done)
-                self.go(f"ks{tile}", ss, sr, "k")
-
-        def a2(self, _):
+            ss, sr = self.q.ss.at[self.kind, tile], self.q.sr.at[self.kind, tile]
+
+            def done(cols, value):
+                ss[:, cols] = value.astype(BF)
+
+            self.into_hidden(1, tile, done)
+            self.go(f"ks{tile}", ss, sr, "k")
+
+        def a2(self, tile):
             need(1 if self.forward else 2, 0)
             t, size = self.q.t, 2 * self.q.t
-            h0, h1 = (0, t), (t, t)
-            for tile in range(self.q.tiles):
-                c, sr = self.q.c.at[self.kind, tile], self.q.sr.at[self.kind, tile]
-                ra = self.q.ra.at[self.kind, tile]
+            c, sr, ra = (buf.at[self.kind, tile] for buf in (self.q.c, self.q.sr, self.q.ra))
+
+            def done(cols, value):
                 self.got(f"ks{tile}")
-
-                def done(cols, value):
-                    c[:, cols] = (value + sr[:, cols].astype(F32)).astype(BF)
-
-                self.into_hidden(0, tile, done)
-                self.go(f"rap{tile}", c.at[rows(yo, size, h0)], ra.at[0], "y+")
-                self.go(f"ram{tile}", c.at[rows(yo, size, h1)], ra.at[1], "y-")
+                c[:, cols] = (value + sr[:, cols].astype(F32)).astype(BF)
+
+            self.into_hidden(0, tile, done)
+            self.go(f"rap{tile}", c.at[rows(yo, size, (0, t))], ra.at[0], "y+")
+            self.go(f"ram{tile}", c.at[rows(yo, size, (t, t))], ra.at[1], "y-")
 
         def rs1(self, tile):
             t, size = self.q.t, 2 * self.q.t
@@ -339,7 +351,7 @@
                 getattr(pair, f"{name}{slot}") for name in ("p", "rx", "rza", "rzb", "rh")
             )
             self.tag = f"o{pair.n}{slot}"
-            self.up, self.up_rest, self.down, self.down_rest = pair.ways(slot)
+            self.up, self.up_rest, self.down, self.down_rest = pair.ways(slot, pair.out_straight[slot])
 
         def go(self, name, src, dst, target):
             go(self.tag + name, src, dst, target)
@@ -407,26 +419,28 @@
                 total = value if total is None else total + value
             return total
 
-        def b(self, _):
+        def b(self, out):
             for which in (1, 2):
                 for half in (0, 1):
                     need(which, half)
-            for tile in range(self.q.tiles):
-                self.got(*(f"k{i}{tile}" for i in range(5)))
-            for out in range(self.number):
-                p = self.p.at[out]
-
-                def tile_of(kind):
-                    for at in range(out * self.wide, (out + 1) * self.wide, TN):
-                        total = self.product(kind, 0, at) + self.product(kind, 1, at)
-                        p[:, pl.ds(at - out * self.wide, TN)] = total.astype(BF)
-
-                pl.when(self.kind == FORWARD)(functools.partial(tile_of, FORWARD))
-                pl.when(self.kind == BACKWARD)(functools.partial(tile_of, BACKWARD))
-                t = self.q.t
-                self.go(f"x1{out}", p.at[rows(row_id(2, 1), t)], self.rx.at[out, 0], "x")
-                self.go(f"zap{out}", p.at[rows(row_id(1, 1), t)], self.rza.at[out, 0], "z+")
-                self.go(f"zam{out}", p.at[rows(row_id(-1, 1), t)], self.rza.at[out, 1], "z-")
+            settle(30)
+            waits = [copies.pop(f"{self.tag}k{i}{tile}") for tile in range(self.q.tiles) for i in range(5)] if out == 0 else []
+            p, t = self.p.at[out], self.q.t
+
+            def tile_of(kind):
+                for at in range(out * self.wide, (out + 1) * self.wide, TN):
+                    total = self.product(kind, 0, at)
+                    if at == 0:
+                        for copy in waits:
+                            copy.wait_recv()
+                    total = total + self.product(kind, 1, at)
+                    p[:, pl.ds(at - out * self.wide, TN)] = total.astype(BF)
+
+            pl.when(self.kind == FORWARD)(functools.partial(tile_of, FORWARD))
+            pl.when(self.kind == BACKWARD)(functools.partial(tile_of, BACKWARD))
+            self.go(f"x1{out}", p.at[rows(row_id(2, 1), t)], self.rx.at[out, 0], "x")
+            self.go(f"zap{out}", p.at[rows(row_id(1, 1), t)], self.rza.at[out, 0], "z+")
+            self.go(f"zam{out}", p.at[rows(row_id(-1, 1), t)], self.rza.at[out, 1], "z-")
 
         def rr1(self, out):
             self.give_sum(f"zbpe{out}", out, row_id(1, 0), self.up_rest, 0, "z+")
@@ -448,6 +462,8 @@
             for name, part, target in (("zhp", self.up, "z+"), ("zhm", self.down, "z-")):
                 if part is not None:
                     self.go(f"{name}{out}", p.at[rows(far, t, part)], self.rh.at[out, pl.ds(*part)], target)
+            if self.q.out_straight[self.slot]:
+                self.go(f"z2{out}", p.at[rows(far, t)], self.rh.at[out], "z2")
 
         def rr2b(self, out):
             t, p, peer = self.q.t, self.p.at[out], row_id(0, 1)
@@ -457,6 +473,7 @@
 
         def rr3(self, out):
             t, p, rh = self.q.t, self.p.at[out], self.rh.at[out]
+            settle(16)
             if self.up is not None:
                 self.got(f"zhp{out}")
                 add_into(p, row_id(1, 0) * t + self.up[0], [(rh, self.up[0])], self.up[1])
@@ -468,7 +485,7 @@
 
         def rr4(self, out):
             t, wide = self.q.t, self.wide
-            self.got(*(f"{name}{out}" for name in ("zbpe", "zbme", "zbp", "zbm", "x2")))
+            self.got(*(f"{name}{out}" for name in ("zbpe", "zbme", "zbp", "zbm", "x2", "z2")))
             mine = rows(row_id(0, 0), t)
             cols = pl.ds(out * wide, wide)
             total = (
@@ -478,6 +495,8 @@
                 + self.rx[out, 1].astype(F32)
                 + self.q.x[self.kind, mine, cols].astype(F32)
             )
+            if self.q.out_straight[self.slot]:
+                total = total + self.rh[out].astype(F32)
             total = total + jnp.where(self.kind == FORWARD, b_out[:, cols], 0.0)
             if self.slot == STAYS:
                 stayed[pl.ds(self.q.first, t), cols] = total.astype(BF)
@@ -512,8 +531,7 @@
     for step in ORDER:
         phase, job = PHASES[step // 32], jobs[step // 8 % 4][step // 2 % 4]
         getattr(job, phase)(step % 2)
-    for copy in pending:
-        copy.wait_send()
+    settle(0)
 
 
 def finish_kernel(came, stayed, signs, handed, leaving):

time: 107 us -> 101 us (0.944)
  Pallas kernels: 106 us -> 100 us
    pallas_call x1, Pallas kernels: 105 us -> 98.1 us  [on_device(): pl.pallas_call(functools.partial(kernel, tuple(scratch)), out_shape=(tile...]
where the time goes in v2:
time: 101 us
  Pallas kernels  100 us (99%)
    pallas_call x1, Pallas kernels, on_device(): pl.pallas_call(functools.partial(kernel, tuple(scratch)), out_shape=(tile...  98.1 us

profile of v2, /device:TPU:0, one launch (start us, length us, event | category | flops | bytes accessed | tf_op | source)
XLA Modules:
  0.0 100.7 jit_solution(5188482125005676453)
XLA Ops:
  0.6 98.1 %feed_forward.1 = (bf16[64,1536]{1,0:T(8,128)(2,1)}, bf16[64,1536]{1,0:T(8,128)(2,1)}) custom-call(bf16[1,64,1536]{2,1,0:T(8,128)(2,1)} %refs_0_.1, bf16[1,64,1536]{2,1,0:T(8,128)(2,1)} %refs_1_.1, bf16[1,1536,3072]{2,1,0:T(8,128)(2,1)} %refs_2_.1, f32[1,3072]{1,0:T(1,128)} %refs_3_.1, bf16[1,3072,1536]{2,1,0:T(8,128)(2,1)} %refs_4_.1, f32[1,1536]{1,0:T(1,128)} %refs_5_.1, ...), custom_call_target="tpu_custom_call" | custom-call | flops 19499999232 | bytes 20000000 | tf_op jit(solution)/shard_map/feed_forward/pallas_call | solution.py:556
  98.8 2.0 %hand_over.1 = (f32[1,64,1536]{2,1,0:T(8,128)}, bf16[1,64,1536]{2,1,0:T(8,128)(2,1)}) custom-call(bf16[64,1536]{1,0:T(8,128)(2,1)} %get-tuple-element.4.came, bf16[64,1536]{1,0:T(8,128)(2,1)} %get-tuple-element.5.stayed, bf16[128,128]{1,0:T(8,128)(2,1)} %constant.2.clone.refs_6_.signs), custom_call_target="tpu_custom_call" | custom-call | tf_op jit(solution)/shard_map/hand_over/pallas_call | solution.py:568

commit v3 on v2

--- a/solution.py
+++ b/solution.py
@@ -26,12 +26,12 @@
     "b", "rr1", "rr2a", "rr2b", "rr3", "rr4", "fin",
 )
 ORDER = (
-    0, 64, 32, 2, 128, 66, 96, 34, 98, 130, 10, 160, 193, 192, 225, 224, 162, 195, 256, 8, 257, 74, 42, 227, 259, 106,
-    288, 194, 289, 138, 72, 291, 226, 258, 321, 40, 323, 357, 359, 104, 320, 136, 170, 391, 389, 202, 290, 421, 234,
-    266, 168, 200, 322, 356, 453, 485, 358, 232, 420, 388, 264, 296, 298, 452, 423, 484, 390, 455, 422, 516, 328, 330,
-    364, 396, 487, 454, 486, 580, 612, 548, 428, 366, 518, 460, 492, 398, 644, 550, 524, 430, 582, 556, 525, 557, 462,
-    614, 676, 494, 620, 646, 588, 652, 526, 621, 589, 527, 653, 708, 558, 622, 590, 678, 684, 685, 591, 623, 559, 654,
-    686, 716, 655, 687,
+    0, 64, 32, 2, 96, 128, 34, 98, 8, 40, 66, 130, 160, 192, 193, 224, 256, 225, 162, 194, 72, 257, 195, 288, 226,
+    258, 10, 42, 227, 259, 136, 104, 290, 74, 289, 320, 291, 106, 322, 356, 388, 358, 168, 321, 390, 138, 200, 323,
+    359, 420, 357, 389, 232, 264, 170, 202, 234, 421, 296, 266, 298, 452, 422, 391, 453, 485, 484, 516, 423, 328, 330,
+    364, 396, 454, 486, 455, 487, 612, 580, 428, 366, 398, 548, 518, 460, 492, 550, 644, 430, 524, 556, 525, 462, 557,
+    494, 582, 588, 620, 526, 589, 621, 527, 558, 653, 676, 590, 654, 652, 622, 646, 684, 614, 685, 591, 559, 623, 686,
+    678, 708, 716, 655, 687,
 )
 
 
@@ -94,9 +94,10 @@
 
 
 def kernel(scratch_names, *refs):
-    tok, cot, w1h, b_in, w2h, b_out, signs_ref, came, stayed = refs[:9]
+    tok, cot, w1h, b_in_h, w2h, b_out_h, signs_h, came, stayed = refs[:9]
     named = dict(zip(scratch_names, refs[9:], strict=True))
     w1, w2, w_sem, send, recv = (named[n] for n in ("w1", "w2", "w_sem", "send", "recv"))
+    b_in, b_out, signs_ref = named["b_in"], named["b_out"], named["signs"]
 
     s, r, col = lax.axis_index("section"), lax.axis_index("row"), lax.axis_index("col")
     z, x, y, k = lax.div(r, 2), lax.rem(r, 2), lax.div(col, 2), lax.rem(col, 2)
@@ -162,6 +163,15 @@
             copy = pltpu.make_async_copy(w2h.at[0, pl.ds(at, W), :], w2.at[half], sem)
         copy.start()
         loads[which, half] = copy
+
+    smalls = [
+        pltpu.make_async_copy(src, dst, w_sem.at[4 + i])
+        for i, (src, dst) in enumerate(((b_in_h, b_in), (b_out_h, b_out), (signs_h, signs_ref)))
+    ]
+
+    def need_smalls():
+        while smalls:
+            smalls.pop().wait()
 
     def need(which, half):
         copy = loads.pop((which, half), None)
@@ -323,6 +333,7 @@
             size, wide = 2 * self.q.t, self.q.wide
             c, rb = self.q.c.at[self.kind, tile], self.q.rb.at[self.kind, tile]
             act, slope = self.q.act.at[self.kind, 0, tile], self.q.slope.at[tile]
+            need_smalls()
             self.got(*(f"{name}{tile}" for name in ("rbpe", "rbme", "rbp", "rbm")))
 
             @pl.loop(0, size // 16)
@@ -516,12 +527,14 @@
             self.got(*(f"sec{out}" for out in range(self.number)))
             came[pl.ds(self.q.first, self.q.t), :] = self.q.inn[...]
 
-    for which, half in ((1, 1), (1, 0), (2, 1), (2, 0)):
-        load_weights(which, half)
-
     barrier = pltpu.get_barrier_semaphore()
     for target in to.values():
         pl.semaphore_signal(barrier, inc=1, device_id=target, device_id_type=pl.DeviceIdType.MESH)
+    for which, half in ((1, 1), (1, 0), (2, 1), (2, 0)):
+        load_weights(which, half)
+    for copy in smalls:
+        copy.start()
+
     pl.semaphore_wait(barrier, len(to))
 
     jobs = []
@@ -544,7 +557,10 @@
     scratch = dict(
         w1=pltpu.VMEM((2, W, W), BF),
         w2=pltpu.VMEM((2, W, W), BF),
-        w_sem=pltpu.SemaphoreType.DMA((4,)),
+        w_sem=pltpu.SemaphoreType.DMA((7,)),
+        b_in=pltpu.VMEM(b_in.shape, F32),
+        b_out=pltpu.VMEM(b_out.shape, F32),
+        signs=pltpu.VMEM((HB, HB), BF),
         send=pltpu.SemaphoreType.DMA((SEMAPHORES,)),
         recv=pltpu.SemaphoreType.DMA((SEMAPHORES,)),
     )
@@ -556,7 +572,7 @@
     came, stayed = pl.pallas_call(
         functools.partial(kernel, tuple(scratch)),
         out_shape=(tile, tile),
-        in_specs=[anywhere, anywhere, anywhere, vmem, anywhere, vmem, vmem],
+        in_specs=[anywhere] * 7,
         out_specs=(vmem, vmem),
         scratch_shapes=list(scratch.values()),
         cost_estimate=pl.CostEstimate(flops=19_500_000_000, bytes_accessed=20_000_000, transcendentals=200_000),

time: 101 us -> 102 us (level)
  no operation moved by 1% of the time
where the time goes in v3:
time: 102 us
  Pallas kernels  101 us (99%)
    pallas_call x1, Pallas kernels, on_device(): pl.pallas_call(functools.partial(kernel, tuple(scratch)), out_shape=(tile...  99 us

profile of v3, /device:TPU:0, one launch (start us, length us, event | category | flops | bytes accessed | tf_op | source)
XLA Modules:
  0.0 101.6 jit_solution(9790196570326783140)
XLA Ops:
  0.6 99.0 %feed_forward.1 = (bf16[64,1536]{1,0:T(8,128)(2,1)}, bf16[64,1536]{1,0:T(8,128)(2,1)}) custom-call(bf16[1,64,1536]{2,1,0:T(8,128)(2,1)} %refs_0_.1, bf16[1,64,1536]{2,1,0:T(8,128)(2,1)} %refs_1_.1, bf16[1,1536,3072]{2,1,0:T(8,128)(2,1)} %refs_2_.1, f32[1,3072]{1,0:T(1,128)} %refs_3_.1, bf16[1,3072,1536]{2,1,0:T(8,128)(2,1)} %refs_4_.1, f32[1,1536]{1,0:T(1,128)} %refs_5_.1, ...), custom_call_target="tpu_custom_call" | custom-call | flops 19499999232 | bytes 20000000 | tf_op jit(solution)/shard_map/feed_forward/pallas_call | solution.py:572
  99.7 2.0 %hand_over.1 = (f32[1,64,1536]{2,1,0:T(8,128)}, bf16[1,64,1536]{2,1,0:T(8,128)(2,1)}) custom-call(bf16[64,1536]{1,0:T(8,128)(2,1)} %get-tuple-element.4.came, bf16[64,1536]{1,0:T(8,128)(2,1)} %get-tuple-element.5.stayed, bf16[128,128]{1,0:T(8,128)(2,1)} %constant.2.clone.refs_6_.signs), custom_call_target="tpu_custom_call" | custom-call | tf_op jit(solution)/shard_map/hand_over/pallas_call | solution.py:584
